TPU v7x, 128 devices: a whole 4x4x4 slice. The times are simulated.
128 devices in a mesh: row: 32 (over x, z, y_lo), col: 4 (over y_hi, core).
Axes of the slice: x: 4, y: 4 (y_hi: 2, y_lo: 2; y = y_hi * 2 + y_lo), z: 4, core: 2. Of those that a mesh axis runs over, the one named last changes fastest.
Arguments:
- contrib: float32 [2, 8192, 8192], P(None, 'row', 'col'), may hold values from -4 to 4
- target_rows: int32 [2, 8192], P(None, 'row'), may hold values from 0 to 8191, as said below
- diag_shift: float32 [2, 1, 32, 256], P(None, None, 'row'), may hold values from 300 to 600
- pattern: int32 [2, 32], replicated, may hold values 0 or 1
Outputs:
- factored: float32 [2, 1, 32, 256, 8, 4, 256], P(None, None, 'row', None, None, 'col')
Inputs may be any that keep to these rules, and one draw needn't show every extreme that they name: `target_rows`: each entry is a row of its front. Call the grid row of a front row i the value (i // 256) modulo the size of the row axis. Of the 256 rows of one row-axis index (an aligned block of one front), at most 16 have targets on any one grid row; in each front one grid row receives exactly 16 from every index.
All inputs are finite; a program needn't handle non-finite values.
Results may differ from a plain program's by a relative error of at most 0.00005.
Values sent between devices are 32-bit elements; how exact they have to be, the bound alone decides.
No kernel may reach another device: no remote copies, remote signals or barrier semaphores. Data moves between devices by JAX's collectives and lax.ppermute only.
A program may use at most 256 MiB of HBM per device.

v0:
```python
import jax
import jax.numpy as jnp
from jax import lax
from jax.sharding import PartitionSpec as P

F = 8192
P_SIZE = 1024
BS = 256


def spread_2(value, axis, source):
    kept = jnp.where(lax.axis_index(axis) == source, value, 0).astype(value.dtype)
    return lax.psum(kept, axis)


def build_sends(contrib_rows, targets, per_owner, owners, local_rows):
    owner_index = targets // BS % owners
    local_index = targets // BS // owners * BS + targets % BS
    matches = (owner_index[:, None] == jnp.arange(owners, dtype=jnp.int32)[None, :]).astype(
        jnp.int32
    )
    rank_within = jnp.sum((jnp.cumsum(matches, axis=0) - 1) * matches, axis=1)
    slot_index = owner_index * per_owner + rank_within
    row_width = contrib_rows.shape[1]
    sends = jnp.zeros((owners * per_owner, row_width), jnp.float32).at[slot_index].set(contrib_rows)
    where_to = (
        jnp.full((owners * per_owner,), local_rows, jnp.int32).at[slot_index].set(local_index)
    )
    return (sends.reshape(owners, per_owner, row_width), where_to.reshape(owners, per_owner))


def add_rows(received, where_to, local_rows):
    row_width = received.shape[-1]
    return (
        jnp.zeros((local_rows, row_width), jnp.float32)
        .at[where_to.reshape(-1)]
        .add(received.reshape(-1, row_width), mode="drop")
    )


def shards(contrib, target_rows, diag_shift, pattern):
    owners = lax.axis_size("row")
    columns = lax.axis_size("col")
    my_row = lax.axis_index("row")
    my_col = lax.axis_index("col")
    per_owner = 2 * contrib.shape[1] // owners
    local_rows = F // owners
    local_cols = F // columns
    col_groups = local_cols // (BS * columns)
    panel_blocks = P_SIZE // BS
    panel_local = P_SIZE // columns
    sends, where_to = jax.vmap(
        lambda rows_in, aims: build_sends(rows_in, aims, per_owner, owners, local_rows)
    )(contrib, target_rows)
    received, got_marks = (
        lax.all_to_all(sends, "row", split_axis=1, concat_axis=1, tiled=True),
        lax.all_to_all(where_to, "row", split_axis=1, concat_axis=1, tiled=True),
    )
    assembled = jax.vmap(lambda rows_in, aims: add_rows(rows_in, aims, local_rows))(
        received, got_marks
    )
    assembled = assembled.reshape(2, local_rows, col_groups, columns, BS)
    front_rows = lax.all_to_all(assembled, "col", split_axis=3, concat_axis=2, tiled=True).reshape(
        2, local_rows, local_cols
    )
    row_steps = jnp.arange(local_rows, dtype=jnp.int32)
    col_steps = jnp.arange(local_cols, dtype=jnp.int32)
    row_global = (row_steps // BS * owners + my_row) * BS + row_steps % BS
    col_global = (col_steps // BS * columns + my_col) * BS + col_steps % BS
    shifts = diag_shift.reshape(2, local_rows)
    front_rows = front_rows + jnp.where(
        row_global[None, :, None] == col_global[None, None, :], shifts[:, :, None], 0.0
    )
    blocks = jnp.arange(F // BS, dtype=jnp.int32)

    def keep_of(positions):
        matches = positions[:, None] // BS == blocks[None, :]
        looked_up = jnp.sum(jnp.where(matches[None], pattern[:, None, :], 0), axis=2)
        return jnp.where(positions[None] // BS < panel_blocks, 1.0, looked_up.astype(jnp.float32))

    keep_rows = keep_of(row_global)
    keep_cols = keep_of(col_global)
    front_rows = front_rows * jnp.where(
        col_global[None, None, :] < P_SIZE, keep_rows[:, :, None], 1.0
    )
    front_rows = front_rows * jnp.where(
        row_global[None, :, None] < P_SIZE, keep_cols[:, None, :], 1.0
    )
    panel_heads = []
    for root_index in range(panel_blocks):
        panel_heads.append(spread_2(front_rows, "row", root_index))
    across = jnp.concatenate(panel_heads, axis=1)
    own_cols, corner_cols = (
        lax.all_gather(front_rows[:, :, :panel_local], "col", axis=2, tiled=True),
        lax.all_gather(across[:, :, :panel_local], "col", axis=2, tiled=True),
    )

    def regroup(gathered):
        leading = gathered.shape[:-1]
        spread = gathered.reshape(leading + (columns, panel_local // BS, BS))
        return jnp.swapaxes(spread, -3, -2).reshape(leading + (P_SIZE,))

    own_cols = regroup(own_cols)
    corner_cols = regroup(corner_cols)

    def factor(whole_rows, left_part, corner, top_rows):
        lower_factor = jnp.linalg.cholesky(0.5 * (corner + corner.T))
        left_factor = jax.scipy.linalg.solve_triangular(lower_factor, left_part.T, lower=True).T
        own_top = lax.dynamic_slice_in_dim(
            lower_factor, jnp.minimum(my_row, panel_blocks - 1) * BS, BS, 0
        )
        head_rows = jnp.where(my_row < panel_blocks, own_top, left_factor)
        left_factor = jnp.concatenate([head_rows, left_factor[BS:]], axis=0)
        upper_factor = jax.scipy.linalg.solve_triangular(
            lower_factor, top_rows[:, panel_local:], lower=True
        )
        schur = whole_rows[:, panel_local:] - jnp.dot(
            left_factor, upper_factor, precision=lax.Precision.HIGHEST
        )
        remainder = jnp.where(row_global[:, None] < P_SIZE, whole_rows[:, panel_local:], schur)
        own_panel = left_factor.reshape(local_rows, panel_local // BS, columns, BS)
        own_panel = lax.dynamic_index_in_dim(own_panel, my_col, 2, keepdims=False).reshape(
            local_rows, panel_local
        )
        return jnp.concatenate([own_panel, remainder], axis=1)

    result = jax.vmap(factor)(front_rows, own_cols, corner_cols, across)
    return result.reshape(2, local_rows // BS, 1, BS, local_cols // BS, 1, BS)


def solution(mesh):
    in_specs = (P(None, "row", "col"), P(None, "row"), P(None, None, "row", None), P())
    out_specs = P(None, None, "row", None, None, "col", None)
    return jax.shard_map(shards, mesh=mesh, in_specs=in_specs, out_specs=out_specs, check_vma=False)
```

profile of v0, /device:TPU:6, one launch (start us, length us, event | category | flops | bytes accessed | tf_op | source)
XLA Modules:
  0.0 2028.0 jit_solution(12585772934278180265)
XLA Ops:
  8.9 24.5 %scatter_fusion = s32[2,512]{1,0:T(2,128)S(1)} fusion(s32[2,512]{1,0:T(2,128)S(1)} %broadcast.1139, s32[512]{0:T(512)S(1)} %bitcast.209, s32[512]{0:T(512)S(1)} %bitcast.226), kind=kCustom, calls=%fused_computation | custom fusion | bytes 10240 | tf_op jit(solution)/shard_map/vmap()/scatter | solution.py:27
  47.9 91.9 %scatter_fusion.1 = f32[2,512,2048]{2,1,0:T(8,128)} fusion(f32[2,512,2048]{2,1,0:T(8,128)} %broadcast_in_dim.181, s32[512]{0:T(512)S(1)} %bitcast.210, f32[512,2048]{1,0:T(8,128)} %bitcast.216), kind=kCustom, calls=%fused_computation.1 | custom fusion | bytes 12587008 | tf_op jit(solution)/shard_map/vmap()/scatter | solution.py:25
  156.4 115.4 %all-to-all-done.1 = f32[2,32,16,2048]{3,2,0,1:T(8,128)} async-done(((f32[2,32,16,2048]{3,2,0,1:T(8,128)}), f32[2,32,16,2048]{3,2,0,1:T(8,128)}, u32[]{:S(2)}, u32[]{:S(2)}) %all-to-all-start.1) | async-done | bytes 8388640 | tf_op jit(solution)/shard_map/all_to_all | solution.py:56
  279.5 17.4 scatter_custom_fusion.2
  315.4 48.7 %all-to-all-done.2 = f32[2,256,2,4,256]{4,2,1,0,3:T(2,128)} async-done(((f32[2,256,2,4,256]{4,2,1,0,3:T(2,128)}), f32[2,256,2,4,256]{4,2,1,0,3:T(2,128)}, u32[]{:S(2)}, u32[]{:S(2)}) %all-to-all-start.2) | async-done | bytes 4194336 | tf_op jit(solution)/shard_map/all_to_all | solution.py:63
  383.3 736.6 %all-reduce.4.cloned.1.call-done = (f32[2,256,2048]{1,2,0:T(8,128)}, f32[2,256,2048]{1,2,0:T(8,128)}, f32[2,256,2048]{1,2,0:T(8,128)}, f32[2,256,2048]{1,2,0:T(8,128)}) async-done(((f32[2,256,2048]{1,2,0:T(8,128)}, f32[2,256,2048]{1,2,0:T(8,128)}, f32[2,256,2048]{1,2,0:T(8,128)}, f32[2,256,2048]{1,2,0:T(8,128)}), (f32[2,256,2048]{1,2,0:T(8,128)}, f32[2,256,2048]{1,2,0:T(8,128)}, f32[2,256,2048]{1,2,0:T(8,128)}, ...) | async-done | bytes 16777232 | tf_op jit(solution)/shard_map/psum | solution.py:13
  1126.1 61.5 %all-gather.3.cloned.1.call-done = f32[2,1024,1024]{1,2,0:T(8,128)} async-done(((f32[2,1024,256]{1,2,0:T(8,128)}), f32[2,1024,1024]{1,2,0:T(8,128)}) %all-gather.3.cloned.1.call-update) | async-done | bytes 8388624 | tf_op jit(solution)/shard_map/all_gather | solution.py:95
  1196.4 12.7 fusion.1
  1217.8 12.0 fusion
  1230.8 23.5 %custom-call.74 = f32[2,128,128]{2,1,0:T(8,128)S(1)} custom-call(f32[2,128,128]{2,1,0:T(8,128)S(1)} %cholesky.578), custom_call_target="Cholesky" | custom-call | tf_op jit(solution)/shard_map/vmap(jit(cholesky))/cholesky | solution.py:107
  1258.5 19.9 custom-call.75
  1285.7 23.5 %custom-call.76 = f32[2,128,128]{2,1,0:T(8,128)S(1)} custom-call(f32[2,128,128]{2,1,0:T(8,128)S(1)} %cholesky.582), custom_call_target="Cholesky" | custom-call | tf_op jit(solution)/shard_map/vmap(jit(cholesky))/cholesky | solution.py:107
  1310.9 19.7 custom-call.77
  1336.7 23.9 %custom-call.78 = f32[2,128,128]{2,1,0:T(8,128)S(1)} custom-call(f32[2,128,128]{2,1,0:T(8,128)S(1)} %cholesky.587), custom_call_target="Cholesky" | custom-call | tf_op jit(solution)/shard_map/vmap(jit(cholesky))/cholesky | solution.py:107
  1361.2 19.7 custom-call.79
  1386.1 23.6 %custom-call.80 = f32[2,128,128]{2,1,0:T(8,128)S(1)} custom-call(f32[2,128,128]{2,1,0:T(8,128)S(1)} %cholesky.592), custom_call_target="Cholesky" | custom-call | tf_op jit(solution)/shard_map/vmap(jit(cholesky))/cholesky | solution.py:107
  1410.5 19.7 custom-call.81
  1435.3 23.5 %custom-call.82 = f32[2,128,128]{2,1,0:T(8,128)S(1)} custom-call(f32[2,128,128]{2,1,0:T(8,128)S(1)} %cholesky.597), custom_call_target="Cholesky" | custom-call | tf_op jit(solution)/shard_map/vmap(jit(cholesky))/cholesky | solution.py:107
  1459.5 19.9 custom-call.83
  1484.3 23.5 %custom-call.84 = f32[2,128,128]{2,1,0:T(8,128)S(1)} custom-call(f32[2,128,128]{2,1,0:T(8,128)S(1)} %cholesky.602), custom_call_target="Cholesky" | custom-call | tf_op jit(solution)/shard_map/vmap(jit(cholesky))/cholesky | solution.py:107
  1508.5 20.1 custom-call.85
  1532.9 23.5 %custom-call.86 = f32[2,128,128]{2,1,0:T(8,128)S(1)} custom-call(f32[2,128,128]{2,1,0:T(8,128)S(1)} %cholesky.607), custom_call_target="Cholesky" | custom-call | tf_op jit(solution)/shard_map/vmap(jit(cholesky))/cholesky | solution.py:107
  1557.1 19.7 custom-call.87
  1580.2 23.6 %custom-call.88 = f32[2,128,128]{2,1,0:T(8,128)S(1)} custom-call(f32[2,128,128]{2,1,0:T(8,128)S(1)} %convolution_subtract_fusion.12), custom_call_target="Cholesky" | custom-call | tf_op jit(solution)/shard_map/vmap(jit(cholesky))/cholesky | solution.py:107
  1605.2 12.5 broadcast_select_fusion
  1617.8 29.9 %while.3 = (s32[]{:T(128)}, f32[2,1024,1024]{2,1,0:T(8,128)}, s32[8,2]{0,1:T(2,128)S(1)}, f32[8,2,128,128]{3,2,0,1:T(8,128)}, s32[]{:T(128)}) while((s32[]{:T(128)}, f32[2,1024,1024]{2,1,0:T(8,128)}, s32[8,2]{0,1:T(2,128)S(1)}, f32[8,2,128,128]{3,2,0,1:T(8,128)}, s32[]{:T(128)}) %tuple.92), condition=%wide.while_cond.1, body=%wide.while_body.1.sunk | while | flops 2 | bytes 263277 | solution.py:108
  1647.6 158.2 %custom-call.89 = f32[2,8,128,128]{2,3,1,0:T(8,128)S(1)} custom-call(f32[2,8,128,128]{3,2,1,0:T(8,128)} %bitcast.230), custom_call_target="InvertDiagBlocksLowerTriangular" | custom-call | tf_op jit(solution)/shard_map/vmap(jit(_solve_triangular))/triangular_solve | solution.py:108
  1879.5 12.3 fusion.26
  1897.1 17.7 convolution_subtract_fusion.2
  1918.6 20.8 %convolution_subtract_fusion.1 = f32[2,128,1792]{1,2,0:T(8,128)S(1)} fusion(f32[2,768,1792]{2,1,0:T(8,128)} %get-tuple-element.70, f32[2,256,2048]{1,2,0:T(8,128)S(1)} %copy-done.4, f32[2,1024,1024]{2,1,0:T(8,128)S(1)} %bitcast.212), kind=kOutput, calls=%fused_computation.36 | convolution fusion | flops 4228317184 | bytes 15466496 | tf_op jit(solution)/shard_map/vmap(jit(_solve_triangular))/triangular_solve | solution.py:114
  1942.4 23.0 %convolution_subtract_fusion = f32[2,128,1792]{1,2,0:T(8,128)} fusion(f32[2,896,1792]{2,1,0:T(8,128)S(1)} %get-tuple-element.66, f32[2,256,2048]{1,2,0:T(8,128)S(1)} %copy-done.4, f32[2,1024,1024]{2,1,0:T(8,128)S(1)} %bitcast.212), kind=kOutput, calls=%fused_computation.35 | convolution fusion | flops 4932960256 | bytes 17432576 | tf_op jit(solution)/shard_map/vmap(jit(_solve_triangular))/triangular_solve | solution.py:114
  1974.9 28.2 %subtract_select_fusion = f32[2,256,1792]{1,2,0:T(8,128)} fusion(f32[2,256,2048]{1,2,0:T(8,128)} %copy-done, f32[2,256,1024]{2,1,0:T(8,128)S(1)} %bitcast_select_fusion, f32[2,1024,1792]{2,1,0:T(8,128)} %convolution_dynamic-update-slice_fusion, pred[256]{0:T(512)(128)(4,1)S(1)} %broadcast_compare_fusion.7), kind=kOutput, calls=%fused_computation.24 | convolution fusion | flops 11276124160 | bytes 24117504 | tf_op jit(solution)/shard_map/vmap()/dot_general | solution.py:117
  (216 shorter events, 293.7 us)
Async XLA Ops:
  34.1 113.4 %all-to-all-start = ((s32[2,32,16]{2,0,1:T(2,128)}), s32[2,32,16]{2,0,1:T(2,128)S(1)}, u32[]{:S(2)}, u32[]{:S(2)}) async-start(s32[2,32,16]{2,0,1:T(2,128)} %copy.274), calls=%async_computation | async-start | bytes 65536 | tf_op jit(solution)/shard_map/all_to_all | solution.py:57
  147.5 8.7 copy-start.14
  147.5 8.8 copy-start.15
  147.5 124.3 %all-to-all-start.1 = ((f32[2,32,16,2048]{3,2,0,1:T(8,128)}), f32[2,32,16,2048]{3,2,0,1:T(8,128)}, u32[]{:S(2)}, u32[]{:S(2)}) async-start(f32[2,32,16,2048]{3,2,0,1:T(8,128)} %copy.276), calls=%async_computation.1 | async-start | bytes 16777216 | tf_op jit(solution)/shard_map/all_to_all | solution.py:56
  309.3 5.1 copy-start.13
  309.3 5.2 copy-start.12
  309.3 54.7 %all-to-all-start.2 = ((f32[2,256,2,4,256]{4,2,1,0,3:T(2,128)}), f32[2,256,2,4,256]{4,2,1,0,3:T(2,128)}, u32[]{:S(2)}, u32[]{:S(2)}) async-start(f32[2,256,2,4,256]{4,2,1,0,3:T(2,128)} %copy.278), calls=%async_computation.2 | async-start | bytes 8388608 | tf_op jit(solution)/shard_map/all_to_all | solution.py:63
  314.3 805.6 %all-reduce.4.cloned.1.call-start = ((), (), s32[]{:S(2)}) async-start(), calls=%async_computation.5 | async-start | bytes 33554432 | tf_op jit(solution)/shard_map/psum | solution.py:13
  377.4 5.8 copy-start
  383.2 804.4 %all-gather.3.cloned.1.call-start = ((), (), s32[]{:S(2)}) async-start(), calls=%async_computation.3 | async-start | bytes 10485760 | tf_op jit(solution)/shard_map/all_gather | solution.py:95
  1123.0 682.9 %all-gather.5.cloned.1.call-start = ((), (), s32[]{:S(2)}) async-start(), calls=%async_computation.4 | async-start | bytes 2621440 | tf_op jit(solution)/shard_map/all_gather | solution.py:94
  1843.5 10.4 slice-start
  1848.7 5.2 slice-start.1
  1848.7 5.2 copy-start.2
  1874.4 5.0 copy-start.1
  1897.1 17.7 copy-start.3
  1914.8 3.7 copy-start.4
  1942.4 23.0 %copy-start.5 = (f32[2,1024,256]{1,2,0:T(8,128)S(1)}, f32[2,1024,256]{1,2,0:T(8,128)}, u32[]{:S(2)}) copy-start(f32[2,1024,256]{1,2,0:T(8,128)} %constant_dynamic-update-slice_fusion.24) | copy-start | bytes 6291460
  1942.4 23.0 %copy-start.6 = (f32[2,128,256]{1,2,0:T(8,128)S(1)}, f32[2,128,256]{1,2,0:T(8,128)}, u32[]{:S(2)}) copy-start(f32[2,128,256]{1,2,0:T(8,128)} %copy.315) | copy-start | bytes 786436
  1942.4 23.1 %copy-start.7 = (f32[2,128,256]{1,2,0:T(8,128)S(1)}, f32[2,128,256]{1,2,0:T(8,128)}, u32[]{:S(2)}) copy-start(f32[2,128,256]{1,2,0:T(8,128)} %copy.316) | copy-start | bytes 786436
  1942.4 23.1 %copy-start.8 = (f32[2,128,256]{1,2,0:T(8,128)S(1)}, f32[2,128,256]{1,2,0:T(8,128)}, u32[]{:S(2)}) copy-start(f32[2,128,256]{1,2,0:T(8,128)} %copy.317) | copy-start | bytes 786436
  1942.4 23.2 %copy-start.9 = (f32[2,128,256]{1,2,0:T(8,128)S(1)}, f32[2,128,256]{1,2,0:T(8,128)}, u32[]{:S(2)}) copy-start(f32[2,128,256]{1,2,0:T(8,128)} %copy.318) | copy-start | bytes 786436
  1942.4 23.2 %copy-start.10 = (f32[2,128,256]{1,2,0:T(8,128)S(1)}, f32[2,128,256]{1,2,0:T(8,128)}, u32[]{:S(2)}) copy-start(f32[2,128,256]{1,2,0:T(8,128)} %copy.319) | copy-start | bytes 786436
  1942.4 23.2 %copy-start.11 = (f32[2,128,256]{1,2,0:T(8,128)S(1)}, f32[2,128,256]{1,2,0:T(8,128)}, u32[]{:S(2)}) copy-start(f32[2,128,256]{1,2,0:T(8,128)} %copy.320) | copy-start | bytes 786436
Sparse Core Ops, SparseCore 0:
  383.3 736.4 all-reduce.3
  1123.1 64.4 all-gather.2
  1189.3 26.0 all-gather.4
where the time goes:
time: 2040 us; the launch traced here: 2030 us
  waiting for transfers between devices  962 us (47%)
  other arithmetic  570 us (28%)
  local copies, waits for them, and re-layouts  237 us (12%)
  matrix products  222 us (11%)
  starting transfers between devices  23.1 us (1%)
    psum x1, waiting for transfers between devices, spread_2(): return lax.psum(kept, axis)  737 us
    another operation x30, other arithmetic, factor(): lower_factor = jnp.linalg.cholesky(0.5 * (corner + corner.T))  332 us
    another operation x3, other arithmetic, factor(): jax.scipy.linalg.solve_triangular(lower_factor, left_part.T, lower=True)  171 us
    another operation x15, matrix products, factor(): jax.scipy.linalg.solve_triangular(lower_factor, top_rows[:, panel_local:]...  133 us
    all_to_all x1, waiting for transfers between devices, shards(): lax.all_to_all(sends, 'row', split_axis=1, concat_axis=1, tiled=True)  115 us
    scatter x1, local copies, waits for them, and re-layouts, build_sends(): jnp.zeros((owners * per_owner, row_width), jnp.float32).at[slot_index]  91.9 us
    all_gather x1, waiting for transfers between devices, shards(): lax.all_gather(across[:, :, :panel_local], 'col', axis=2, tiled=True)  61.5 us
    all_to_all x1, waiting for transfers between devices, shards(): lax.all_to_all(assembled, 'col', split_axis=3, concat_axis=2, tiled=True)  48.7 us
  transfers between devices with their start and end apart: 6, of which 4 were waited for; matrix products, arithmetic and copies ran while one was open for 36% of the time, Pallas kernels for 0%

commit v1 on v0

v1 whole, which is shorter than its diff:
```python
import jax
import jax.numpy as jnp
from jax import lax
from jax.experimental import pallas as pl
from jax.experimental.pallas import tpu as pltpu
from jax.sharding import PartitionSpec as P

F = 8192
P_SIZE = 1024
BS = 256
HI = lax.Precision.HIGHEST
VM = pl.BlockSpec(memory_space=pltpu.VMEM)
SM = pl.BlockSpec(memory_space=pltpu.SMEM)
F32 = jnp.float32


def params():
    return pltpu.CompilerParams(vmem_limit_bytes=60 * 1024 * 1024)


def dot_nn(a, b):
    return lax.dot_general(a, b, (((1,), (0,)), ((), ())), precision=HI, preferred_element_type=F32)


def dot_nt(a, b):
    return lax.dot_general(a, b, (((1,), (1,)), ((), ())), precision=HI, preferred_element_type=F32)


def dot_tn(a, b):
    return lax.dot_general(a, b, (((0,), (0,)), ((), ())), precision=HI, preferred_element_type=F32)


def build_kernel(pos_ref, t_ref, x_ref, diag_ref, main_ref, panel_ref, marks_ref, buf, cnt):
    my_col = pos_ref[1]
    for f in range(2):
        for j in range(16):
            block, half = j // 2, j % 2
            place = (block % 4) * 4 + (block // 4) * 2 + half
            buf[pl.ds(f * 4096 + place, 256, stride=16), :] = x_ref[f, :, j * 128:(j + 1) * 128]

    def clear(i, _):
        cnt[i] = 0
        for k in range(16):
            marks_ref[i // 2, (i % 2) * 16 + k] = 256
        return 0

    lax.fori_loop(0, 64, clear, 0)
    for i in range(32):
        f = i // 16
        panel_ref[pl.ds(i * 72 + 64, 2), :] = diag_ref[f]
    for f in range(2):

        def place_row(i, _):
            target = t_ref[f, i]
            owner = target // 256
            slot = cnt[f * 32 + owner]
            cnt[f * 32 + owner] = slot + 1
            marks_ref[owner, f * 16 + slot] = target % 256
            source = (f * 256 + i) * 16

            @pl.when(owner >= 4)
            def _():
                for c in range(4):
                    dest = (((owner * 4 + c) * 2 + f) * 16 + slot) * 4
                    main_ref[pl.ds(dest, 4), :] = buf[pl.ds(source + c * 4, 4), :]

            @pl.when(owner < 4)
            def _():
                for c in range(4):
                    q = (c - my_col + 4) % 4
                    for u in range(2):
                        for h in range(2):
                            dest = f * 16 + u * 8 + q * 2 + h
                            panel_ref[pl.ds(dest * 72 + owner * 16 + slot, 1), :] = (
                                buf[pl.ds(source + c * 4 + u * 2 + h, 1), :]
                            )

            return 0

        lax.fori_loop(0, 256, place_row, 0)


def build(pos, targets, contrib, diag):
    return pl.pallas_call(
        build_kernel,
        out_shape=(
            jax.ShapeDtypeStruct((16384, 128), F32),
            jax.ShapeDtypeStruct((32 * 72, 128), F32),
            jax.ShapeDtypeStruct((32, 32), jnp.int32),
        ),
        in_specs=[SM, SM, VM, VM],
        out_specs=(VM, VM, SM),
        scratch_shapes=[pltpu.VMEM((8192, 128), F32), pltpu.SMEM((64,), jnp.int32)],
        compiler_params=params(),
    )(pos, targets, contrib, diag)


def eye128():
    return (
        lax.broadcasted_iota(jnp.int32, (128, 128), 0) == lax.broadcasted_iota(jnp.int32, (128, 128), 1)
    ).astype(F32)


def panel_kernel(pos_ref, marks_ref, pattern_ref, x_ref, out_ref, acc):
    my_row, my_col = pos_ref[0], pos_ref[1]
    f, u, q, h = my_row // 16, (my_row // 8) % 2, (my_row // 2) % 4, my_row % 2
    block = 8 * my_col + u * 4 + (q + my_col) % 4
    for n in range(4):
        acc[n] = jnp.zeros((1032, 128), F32)

    def source(s, _):
        def step(k, _):
            for n in range(4):
                mark = marks_ref[s, 32 + n * 16 + k]
                row = jnp.where(mark == 256, 1024, n * 256 + mark)
                acc[n, pl.ds(row, 1), :] += x_ref[pl.ds(s * 72 + n * 16 + k, 1), :]
            return 0

        return lax.fori_loop(0, 16, step, 0, unroll=4)

    lax.fori_loop(0, 32, source, 0)
    scale = jnp.where(block >= 4, pattern_ref[f, block], 1).astype(F32)
    for n in range(4):
        out_ref[pl.ds(n * 256, 256), :] = acc[n, n * 256:(n + 1) * 256, :] * scale

    @pl.when(block < 4)
    def _():
        start = pl.multiple_of(block * 256 + h * 128, 128)
        shift = x_ref[pl.ds(block * 72 + 64 + h, 1), :]
        out_ref[pl.ds(start, 128), :] += eye128() * shift


def panel_piece(pos, marks, pattern, received):
    return pl.pallas_call(
        panel_kernel,
        out_shape=jax.ShapeDtypeStruct((1024, 128), F32),
        in_specs=[SM, SM, SM, VM],
        out_specs=VM,
        scratch_shapes=[pltpu.VMEM((4, 1032, 128), F32)],
        compiler_params=params(),
    )(pos, marks, pattern, received)


SRCS = 8


def assemble_kernel(pos_ref, marks_ref, pattern_ref, diag_ref, x_ref, out_ref, left_ref, acc):
    step = pl.program_id(0)
    my_row, my_col = pos_ref[0], pos_ref[1]

    @pl.when(step == 0)
    def _():
        acc[...] = jnp.zeros_like(acc)

    def source(s, _):
        def slot(k, _):
            for f in range(2):
                mark = marks_ref[step * SRCS + s, f * 16 + k]

                @pl.when(mark < 256)
                def _():
                    for c in range(4):
                        piece = x_ref[pl.ds((((s * 4 + c) * 2 + f) * 16 + k) * 4, 4), :]
                        acc[f, pl.ds(mark * 16 + c * 4, 4), :] += piece

            return 0

        return lax.fori_loop(0, 16, slot, 0)

    lax.fori_loop(0, SRCS, source, 0)

    @pl.when(step == pl.num_programs(0) - 1)
    def _():
        for f in range(2):
            scale = jnp.where(my_row >= 4, pattern_ref[f, my_row], 1).astype(F32)

            @pl.when(my_row % 4 == my_col)
            def _():
                for h in range(2):
                    at = pl.ds(h * 2048 + (my_row // 4) * 2 + h, 128, stride=16)
                    acc[f, at, :] += eye128() * diag_ref[f, h:h + 1, :]

            for h in range(2):
                left_ref[f, :, h * 128:(h + 1) * 128] = acc[f, pl.ds(h, 256, stride=16), :] * scale
            out_ref[f] = acc[f]


def assemble(pos, marks, pattern, diag, received):
    chunk = SRCS * 512
    return pl.pallas_call(
        assemble_kernel,
        grid=(32 // SRCS,),
        out_shape=(
            jax.ShapeDtypeStruct((2, 4096, 128), F32),
            jax.ShapeDtypeStruct((2, 256, 256), F32),
        ),
        in_specs=[SM, SM, SM, VM, pl.BlockSpec((chunk, 128), lambda s: (s, 0))],
        out_specs=(
            pl.BlockSpec((2, 4096, 128), lambda s: (0, 0, 0)),
            pl.BlockSpec((2, 256, 256), lambda s: (0, 0, 0)),
        ),
        scratch_shapes=[pltpu.VMEM((2, 4096, 128), F32)],
        compiler_params=params(),
    )(pos, marks, pattern, diag, received)


def factor_kernel(pos_ref, c_ref, l_ref, x_ref, d_ref):
    my_row, my_col = pos_ref[0], pos_ref[1]
    lanes = lax.broadcasted_iota(jnp.int32, (8, 128), 1)
    subs = lax.broadcasted_iota(jnp.int32, (8, 128), 0)
    low = lax.broadcasted_iota(jnp.int32, (128, 128), 0) >= lax.broadcasted_iota(jnp.int32, (128, 128), 1)

    def corner(f, rows, block):
        other = jnp.bitwise_xor(block // 2, my_col)
        return c_ref[other % 2, other // 2, f, jnp.bitwise_xor(block % 2, my_row % 2), pl.ds(rows * 128, 128), :]

    def symmetrize(f, _):
        for i in range(8):
            for j in range(i + 1):
                l_ref[f, i * 128:(i + 1) * 128, j * 128:(j + 1) * 128] = 0.5 * (
                    corner(f, i, j) + corner(f, j, i).T
                )
        return 0

    lax.fori_loop(0, 2, symmetrize, 0)
    for p in range(8):
        here = slice(p * 128, (p + 1) * 128)
        for f in range(2):
            d_ref[f, :, :128] = l_ref[f, here, here]
            d_ref[f, :, 128:] = eye128()

        def group(g, _):
            for f in range(2):
                rows = d_ref[f, pl.ds(pl.multiple_of(g * 8, 8), 8), :]
                a8, r8 = rows[:, :128], rows[:, 128:]
                turned = pltpu.roll(a8, (128 - g * 8) % 128, 1)
                cols = [jnp.broadcast_to(turned[:, j:j + 1], (8, 128)) for j in range(8)]
                for j in range(8):
                    pivot = jnp.broadcast_to(cols[j][j:j + 1, :], (8, 128))
                    root = lax.rsqrt(pivot)
                    root = root * (1.5 - 0.5 * pivot * root * root)
                    mult = jnp.where(subs > j, cols[j] * root, 0.0)
                    for k in range(j + 1, 8):
                        cols[k] = cols[k] - mult * (cols[k][j:j + 1, :] * root)
                    ua, ur = a8[j:j + 1, :] * root, r8[j:j + 1, :] * root
                    a8 = jnp.where(subs == j, ua, a8 - mult * ua)
                    r8 = jnp.where(subs == j, ur, r8 - mult * ur)
                new = jnp.concatenate([a8, r8], axis=1)
                d_ref[f, pl.ds(pl.multiple_of(g * 8, 8), 8), :] = new
                later = jnp.where(lanes > g * 8 + 7, a8, 0.0)
                d_ref[f] = d_ref[f] - dot_tn(later, new)
            return 0

        lax.fori_loop(0, 16, group, 0)

        def rest(f, _):
            inverse = jnp.where(low, d_ref[f, :, 128:], 0.0)
            l_ref[f, here, here] = jnp.where(low, d_ref[f, :, :128].T, 0.0)
            x_ref[f, here, here] = inverse
            if p > 0:
                done = p * 128
                both = dot_nn(l_ref[f, here, :done], x_ref[f, :done, :done])
                x_ref[f, here, :done] = -dot_nn(inverse, both)
            if p < 7:
                after = (p + 1) * 128
                l_ref[f, here, after:] = jnp.zeros((128, 1024 - after), F32)
                x_ref[f, here, after:] = jnp.zeros((128, 1024 - after), F32)
                l_ref[f, after:, here] = dot_nt(l_ref[f, after:, here], inverse)
                for i in range(p + 1, 8):
                    mine = slice(i * 128, (i + 1) * 128)
                    upto = slice(after, (i + 1) * 128)
                    l_ref[f, mine, upto] = l_ref[f, mine, upto] - dot_nt(
                        l_ref[f, mine, here], l_ref[f, upto, here]
                    )
            return 0

        lax.fori_loop(0, 2, rest, 0)


def factor(pos, corner):
    return pl.pallas_call(
        factor_kernel,
        out_shape=(
            jax.ShapeDtypeStruct((2, 1024, 1024), F32),
            jax.ShapeDtypeStruct((2, 1024, 1024), F32),
        ),
        in_specs=[SM, VM],
        out_specs=(VM, VM),
        scratch_shapes=[pltpu.VMEM((2, 128, 256), F32)],
        compiler_params=params(),
    )(pos, corner)


def left_kernel(pos_ref, a_ref, x_ref, w_ref, own_ref, wide, factor_rows):
    my_col = pos_ref[1]
    for core in range(2):
        for far in range(2):
            column = jnp.bitwise_xor(my_col, core + 2 * far)
            wide[:, pl.ds(pl.multiple_of(column * 256, 256), 256)] = a_ref[core, far, 0]
    factor_rows[...] = dot_nt(wide[...], x_ref[0])
    w_ref[0] = dot_nn(factor_rows[...], x_ref[0])
    own_ref[0] = factor_rows[:, pl.ds(pl.multiple_of(my_col * 256, 256), 256)]


def left(pos, a, inverse):
    return pl.pallas_call(
        left_kernel,
        grid=(2,),
        out_shape=(
            jax.ShapeDtypeStruct((2, 256, 1024), F32),
            jax.ShapeDtypeStruct((2, 256, 256), F32),
        ),
        in_specs=[
            SM,
            pl.BlockSpec((2, 2, 1, 256, 256), lambda f: (0, 0, f, 0, 0)),
            pl.BlockSpec((1, 1024, 1024), lambda f: (f, 0, 0)),
        ],
        out_specs=(
            pl.BlockSpec((1, 256, 1024), lambda f: (f, 0, 0)),
            pl.BlockSpec((1, 256, 256), lambda f: (f, 0, 0)),
        ),
        scratch_shapes=[pltpu.VMEM((256, 1024), F32), pltpu.VMEM((256, 1024), F32)],
        compiler_params=params(),
    )(pos, a, inverse)


def schur_kernel(pos_ref, front_ref, w_ref, own_ref, lo_ref, hi_ref, out_ref, head):
    j = pl.program_id(1)
    my_row = pos_ref[0]
    par = my_row % 2

    @pl.when(j == 0)
    def _():
        for h in range(2):
            out_ref[0, pl.ds(h, 256, stride=16), :] = own_ref[0, :, h * 128:(h + 1) * 128]

    @pl.when((j > 0) & (my_row >= 4))
    def _():
        for h in range(2):
            y = jnp.bitwise_xor(par, h)
            gone = dot_nn(w_ref[0, :, :512], lo_ref[0, 0, y]) + dot_nn(w_ref[0, :, 512:], hi_ref[0, 0, y])
            at = pl.ds(2 * j + h, 256, stride=16)
            out_ref[0, at, :] = front_ref[0, at, :] - gone

    @pl.when((j > 0) & (my_row < 4))
    def _():
        for h in range(2):
            y = jnp.bitwise_xor(par, h)
            start = pl.multiple_of((my_row % 2) * 256, 256)
            at = pl.ds(2 * j + h, 256, stride=16)

            @pl.when(my_row < 2)
            def _():
                out_ref[0, at, :] = lo_ref[0, 0, y, pl.ds(start, 256), :]

            @pl.when(my_row >= 2)
            def _():
                out_ref[0, at, :] = hi_ref[0, 0, y, pl.ds(start, 256), :]


def schur(pos, front, w, own, lo, hi):
    def where(f, j, pos):
        x, z = f * 2 + j % 2, (pos[1] + 4 - j // 2) % 4
        return (pos[0] // 8 + 4 - x) % 4, ((pos[0] // 2) % 4 + 4 - z) % 4

    def lo_map(f, j, pos):
        x, z = where(f, j, pos)
        return x, z, 0, 0, 0

    def hi_map(f, j, pos):
        x, z = where(f, j, pos)
        return z, x, 0, 0, 0

    return pl.pallas_call(
        schur_kernel,
        grid_spec=pltpu.PrefetchScalarGridSpec(
            num_scalar_prefetch=1,
            grid=(2, 8),
            in_specs=[
                pl.BlockSpec((1, 4096, 128), lambda f, j, pos: (f, 0, 0)),
                pl.BlockSpec((1, 256, 1024), lambda f, j, pos: (f, 0, 0)),
                pl.BlockSpec((1, 256, 256), lambda f, j, pos: (f, 0, 0)),
                pl.BlockSpec((1, 1, 2, 512, 128), lo_map),
                pl.BlockSpec((1, 1, 2, 512, 128), hi_map),
            ],
            out_specs=pl.BlockSpec((1, 4096, 128), lambda f, j, pos: (f, 0, 0)),
            scratch_shapes=[pltpu.VMEM((8, 128), F32)],
        ),
        out_shape=jax.ShapeDtypeStruct((2, 4096, 128), F32),
        compiler_params=params(),
    )(pos, front, w, own, lo, hi)


def turn(axis, by):
    pairs = []
    for x in range(4):
        for z in range(4):
            for y in range(2):
                to = ((x + by) % 4, z) if axis == "x" else (x, (z + by) % 4)
                pairs.append((x * 8 + z * 2 + y, to[0] * 8 + to[1] * 2 + y))
    return pairs


def ring(value, axis):
    forth, back = turn(axis, 1), turn(axis, -1)
    half = value.shape[-2] // 2
    below = lax.ppermute(value, "row", forth)
    above = lax.ppermute(value, "row", back)
    first = lax.ppermute(below[..., :half, :], "row", forth)
    second = lax.ppermute(above[..., half:, :], "row", back)
    return jnp.stack([value, below, jnp.concatenate([first, second], axis=-2), above])


def across(value, pairs, axis):
    return jnp.stack([value, lax.ppermute(value, axis, pairs)])


CORE = [(0, 1), (1, 0), (2, 3), (3, 2)]
FAR = [(0, 2), (2, 0), (1, 3), (3, 1)]
NEAR = [(i, i ^ 1) for i in range(32)]


def shards(contrib, target_rows, diag_shift, pattern):
    my_row = lax.axis_index("row").astype(jnp.int32)
    my_col = lax.axis_index("col").astype(jnp.int32)
    pos = jnp.stack([my_row, my_col])
    diag = diag_shift.reshape(2, 2, 128)
    main, panel, marks = build(pos, target_rows, contrib, diag)
    heads = jnp.swapaxes(marks[:4].reshape(4, 2, 16), 0, 1).reshape(2, 1, 64)
    heads = jnp.broadcast_to(heads, (2, 16, 64)).reshape(32, 64)
    marks = lax.all_to_all(
        jnp.concatenate([marks, heads], axis=1), "row", split_axis=0, concat_axis=0, tiled=True
    )
    panel = lax.all_to_all(panel.reshape(32, 72, 128), "row", split_axis=0, concat_axis=0, tiled=True)
    piece = panel_piece(pos, marks, pattern, panel.reshape(32 * 72, 128))
    moves = [
        (i * 4 + c, i * 4 + ((i // 2) % 4 + c) % 4) for i in range(32) for c in range(4)
    ]
    piece = lax.ppermute(piece, ("row", "col"), moves)
    main = lax.all_to_all(
        main.reshape(128, 128, 128), ("row", "col"), split_axis=0, concat_axis=0, tiled=True
    )
    front, own_left = assemble(pos, marks, pattern, diag, main.reshape(16384, 128))

    pair = across(piece, NEAR, "row")
    lo = ring(ring(pair[:, :512], "z"), "x")
    hi = ring(ring(pair[:, 512:], "x"), "z")

    my_x, my_z = my_row // 8, (my_row // 2) % 4
    z_rel = (my_z + 4 - my_col) % 4
    corner = []
    for f in range(2):
        x_rel = (my_x + 4 - 2 * f) % 4
        low = lax.dynamic_slice(lo, (x_rel, z_rel, 0, 0, 0), (1, 1, 2, 512, 128))
        high = lax.dynamic_slice(hi, (z_rel, x_rel, 0, 0, 0), (1, 1, 2, 512, 128))
        corner.append(jnp.concatenate([low[0, 0], high[0, 0]], axis=1))
    corner = jnp.stack(corner)
    corner = across(across(corner, FAR, "col"), CORE, "col")
    lower, inverse = factor(pos, corner)
    lefts = across(across(own_left, FAR, "col"), CORE, "col")
    w, own = left(pos, lefts, inverse)
    head = lax.dynamic_slice(lower, (0, jnp.minimum(my_row, 3) * 256, my_col * 256), (2, 256, 256))
    own = jnp.where(my_row < 4, head, own)
    result = schur(pos, front, w, own, lo, hi)
    return result.reshape(2, 1, 1, 256, 8, 1, 256)


def solution(mesh):
    in_specs = (P(None, "row", "col"), P(None, "row"), P(None, None, "row", None), P())
    out_specs = P(None, None, "row", None, None, "col", None)
    return jax.shard_map(shards, mesh=mesh, in_specs=in_specs, out_specs=out_specs, check_vma=False)
```

time: 2040 us -> 693 us (0.34)
  waiting for transfers between devices: 962 us -> 209 us
  other arithmetic: 570 us -> 33.1 us
  Pallas kernels: 0 us -> 331 us
  local copies, waits for them, and re-layouts: 237 us -> 13.3 us
  matrix products: 222 us -> 0 us
  blocking collectives: 0 us -> 38 us
  starting transfers between devices: 23.1 us -> 56.6 us
    psum x1 -> x0, waiting for transfers between devices: 737 us -> none  [spread_2(): return lax.psum(kept, axis)]
    another operation x35 -> x17, other arithmetic: 504 us -> 30.3 us  [the longest x8 15.9 us: ring(): jnp.stack([value, below, jnp.concatenate([first, second], axis=-2), above])]
    pallas_call x0 -> x6, Pallas kernels: none -> 331 us  [the longest x1 219 us: factor(): pl.pallas_call(factor_kernel, out_shape=(jax.ShapeDtypeStruct((2, 1024, 1...]
    ppermute x0 -> x22, waiting for transfers between devices: none -> 209 us  [the longest x4 107 us: ring(): above = lax.ppermute(value, 'row', back)]
    another operation x44 -> x0, matrix products: 194 us -> none  [the longest x15 133 us: factor(): jax.scipy.linalg.solve_triangular(lower_factor, top_rows[:, panel_local:]...]
    all_to_all x3 -> x1, waiting for transfers between devices: 164 us -> 0.01 us  [shards(): lax.all_to_all(main.reshape(128, 128, 128), ('row', 'col'), split_axis=0,...]
    scatter x2 -> x0, local copies, waits for them, and re-layouts: 116 us -> none  [the longest x1 91.9 us: build_sends(): jnp.zeros((owners * per_owner, row_width), jnp.float32).at[slot_index]]
    all_gather x2 -> x0, waiting for transfers between devices: 61.5 us -> none  [the longest x1 61.5 us: shards(): lax.all_gather(across[:, :, :panel_local], 'col', axis=2, tiled=True)]
  transfers between devices with their start and end apart: 6 -> 23, of which waited for: 4 -> 10; matrix products, arithmetic and copies ran while one was open for 36% -> 5% of each run, Pallas kernels for 0% -> 3%
where the time goes in v1:
time: 693 us; the launch traced here: 681 us
  Pallas kernels  331 us (48%)
  waiting for transfers between devices  209 us (30%)
  starting transfers between devices  56.6 us (8%)
  blocking collectives  38 us (5%)
  other arithmetic  33.1 us (5%)
  local copies, waits for them, and re-layouts  13.3 us (2%)
    pallas_call x1, Pallas kernels, factor(): pl.pallas_call(factor_kernel, out_shape=(jax.ShapeDtypeStruct((2, 1024, 1...  219 us
    ppermute x4, waiting for transfers between devices, ring(): above = lax.ppermute(value, 'row', back)  107 us
    ppermute x5, waiting for transfers between devices, across(): return jnp.stack([value, lax.ppermute(value, axis, pairs)])  69.9 us
    pallas_call x1, Pallas kernels, schur(): pl.pallas_call(schur_kernel, grid_spec=pltpu.PrefetchScalarGridSpec(num_s...  34.5 us
    pallas_call x1, Pallas kernels, build(): pl.pallas_call(build_kernel, out_shape=(jax.ShapeDtypeStruct((16384, 128)...  27.7 us
    ppermute x4, waiting for transfers between devices, ring(): second = lax.ppermute(above[..., half:, :], 'row', back)  27.1 us
    all_to_all x1, blocking collectives, shards(): lax.all_to_all(panel.reshape(32, 72, 128), 'row', split_axis=0, concat_ax...  22.3 us
    pallas_call x1, Pallas kernels, assemble(): pl.pallas_call(assemble_kernel, grid=(32 // SRCS,), out_shape=(jax.ShapeD...  20 us
  transfers between devices with their start and end apart: 23, of which 10 were waited for; matrix products, arithmetic and copies ran while one was open for 5% of the time, Pallas kernels for 3%

profile of v1, /device:TPU:6, one launch (start us, length us, event | category | flops | bytes accessed | tf_op | source)
XLA Modules:
  0.0 681.1 jit_solution(7185221012126536861)
XLA Ops:
  0.6 27.7 %shard_map.46 = (f32[16384,128]{1,0:T(8,128)}, f32[2304,128]{1,0:T(8,128)}, s32[32,32]{1,0:T(8,128)}) custom-call(s32[2]{0:T(128)} %pad_add_fusion.1.pos_ref, s32[2,256]{1,0:T(2,128)} %t_ref.1, f32[2,256,2048]{2,1,0:T(8,128)} %x_ref.1, f32[2,2,128]{2,1,0:T(2,128)} %bitcast.79), custom_call_target="tpu_custom_call" | custom-call | tf_op jit(solution)/shard_map/pallas_call | solution.py:84
  30.0 15.7 %all_to_all.21 = s32[32,1,96]{2,1,0:T(1,128)} all-to-all(s32[32,1,96]{2,1,0:T(1,128)S(1)} %bitcast.77), channel_id=1, replica_groups=mesh['row'=32,'col'=4] {'row'}, dimensions={0} | all-to-all | bytes 24576 | tf_op jit(solution)/shard_map/all_to_all | solution.py:431
  45.7 22.3 %all_to_all.22 = f32[32,72,128]{2,1,0:T(8,128)} all-to-all(f32[32,72,128]{2,1,0:T(8,128)} %bitcast.68), channel_id=1, replica_groups=mesh['row'=32,'col'=4] {'row'}, dimensions={0} | all-to-all | bytes 2359296 | tf_op jit(solution)/shard_map/all_to_all | solution.py:434
  67.9 12.2 %shard_map.48 = f32[1024,128]{1,0:T(8,128)} custom-call(s32[2]{0:T(128)} %pad_add_fusion.1.pos_ref, s32[32,96]{1,0:T(8,128)} %bitcast.74, s32[2,32]{1,0:T(2,128)} %pattern_ref.3, f32[2304,128]{1,0:T(8,128)} %bitcast.60), custom_call_target="tpu_custom_call" | custom-call | tf_op jit(solution)/shard_map/pallas_call | solution.py:134
  82.8 10.3 %collective-permute-done.3 = f32[1024,128]{1,0:T(8,128)S(1)} collective-permute-done((f32[1024,128]{1,0:T(8,128)S(1)}, f32[1024,128]{1,0:T(8,128)S(1)}, u32[]{:S(2)}, u32[]{:S(2)}) %collective-permute-start.3) | collective-permute-done | bytes 524320 | tf_op jit(solution)/shard_map/ppermute | solution.py:415
  93.8 2.7 collective-permute-start.12
  96.5 12.8 %collective-permute-start.6 = (f32[2,512,128]{2,1,0:T(8,128)S(1)}, f32[2,512,128]{2,1,0:T(8,128)S(1)}, u32[]{:S(2)}, u32[]{:S(2)}) collective-permute-start(f32[2,512,128]{2,1,0:T(8,128)S(1)} %get-tuple-element.35), channel_id=1, source_target_pairs={{0,24},{4,28},{8,0},{12,4},{16,8},{20,12},{24,16},{28,20},{32,56},... | collective-permute-start | bytes 1572872 | tf_op jit(solution)/shard_map/ppermute | solution.py:408
  109.4 3.3 collective-permute-start.13
  112.7 7.7 %collective-permute-done.6 = f32[2,512,128]{2,1,0:T(8,128)S(1)} collective-permute-done((f32[2,512,128]{2,1,0:T(8,128)S(1)}, f32[2,512,128]{2,1,0:T(8,128)S(1)}, u32[]{:S(2)}, u32[]{:S(2)}) %collective-permute-start.6) | collective-permute-done | bytes 524320 | tf_op jit(solution)/shard_map/ppermute | solution.py:408
  120.4 4.5 collective-permute-start.7
  126.9 5.4 collective-permute-start.18
  133.2 2.4 fusion.5
  135.6 3.2 collective-permute-start.8
  138.9 7.7 %all-to-all-start.1 = ((f32[128,128,128]{2,1,0:T(8,128)}), f32[128,128,128]{2,1,0:T(8,128)}, u32[]{:S(2)}, u32[]{:S(2)}) async-start(f32[128,128,128]{2,1,0:T(8,128)} %bitcast.59), calls=%async_computation.1 | async-start | bytes 16777216 | tf_op jit(solution)/shard_map/all_to_all | solution.py:440
  146.5 99.5 %collective-permute-done.18 = f32[4,2,512,128]{3,2,1,0:T(8,128)} collective-permute-done((f32[4,2,512,128]{3,2,1,0:T(8,128)}, f32[4,2,512,128]{3,2,1,0:T(8,128)}, u32[]{:S(2)}, u32[]{:S(2)}) %collective-permute-start.18) | collective-permute-done | bytes 2097184 | tf_op jit(solution)/shard_map/ppermute | solution.py:408
  251.7 2.3 slice.49
  256.3 6.5 collective-permute-start.9
  262.8 25.7 %collective-permute-done.19 = f32[4,2,256,128]{3,2,1,0:T(8,128)} collective-permute-done((f32[4,2,256,128]{3,2,1,0:T(8,128)S(1)}, f32[4,2,256,128]{3,2,1,0:T(8,128)}, u32[]{:S(2)}, u32[]{:S(2)}) %collective-permute-start.19) | collective-permute-done | bytes 1048608 | tf_op jit(solution)/shard_map/ppermute | solution.py:410
  288.5 3.5 collective-permute-done.17
  296.9 2.7 pad_maximum_fusion.1.hi_ref
  299.7 5.5 pad_maximum_fusion.lo_ref
  305.9 2.6 copy-done.1
  310.7 43.7 %collective-permute-done.20 = f32[2,2,1024,128]{3,2,1,0:T(8,128)S(1)} collective-permute-done((f32[2,2,1024,128]{3,2,1,0:T(8,128)S(1)}, f32[2,2,1024,128]{3,2,1,0:T(8,128)S(1)}, u32[]{:S(2)}, u32[]{:S(2)}) %collective-permute-start.20) | collective-permute-done | bytes 2097184 | tf_op jit(solution)/shard_map/ppermute | solution.py:415
  354.5 4.2 fusion.3
  358.7 20.0 %shard_map.47 = (f32[2,4096,128]{2,1,0:T(8,128)}, f32[2,256,256]{2,1,0:T(8,128)}) custom-call(s32[2]{0:T(128)} %pad_add_fusion.1.pos_ref, s32[32,96]{1,0:T(8,128)} %bitcast.75, s32[2,32]{1,0:T(2,128)} %pattern_ref.3, f32[2,2,128]{2,1,0:T(2,128)} %bitcast.80, f32[16384,128]{1,0:T(8,128)} %bitcast.8.x_ref), custom_call_target="tpu_custom_call" | custom-call | tf_op jit(solution)/shard_map/pallas_call | solution.py:190
  378.6 2.7 collective-permute-start
  381.3 13.2 %collective-permute-done = f32[2,256,256]{2,1,0:T(8,128)S(1)} collective-permute-done((f32[2,256,256]{2,1,0:T(8,128)}, f32[2,256,256]{2,1,0:T(8,128)S(1)}, u32[]{:S(2)}, u32[]{:S(2)}) %collective-permute-start) | collective-permute-done | bytes 524320 | tf_op jit(solution)/shard_map/ppermute | solution.py:415
  395.8 2.6 collective-permute-done.1
  401.4 6.3 pad_maximum_fusion.2.c_ref
  407.7 218.9 %shard_map.49 = (f32[2,1024,1024]{2,1,0:T(8,128)}, f32[2,1024,1024]{2,1,0:T(8,128)}) custom-call(s32[2]{0:T(128)} %pad_add_fusion.1.pos_ref, f32[2,2,2,2,1024,128]{5,4,3,2,1,0:T(8,128)} %pad_maximum_fusion.2.c_ref), custom_call_target="tpu_custom_call" | custom-call | tf_op jit(solution)/shard_map/pallas_call | solution.py:281
  626.6 17.8 %shard_map.50 = (f32[2,256,1024]{2,1,0:T(8,128)}, f32[2,256,256]{2,1,0:T(8,128)}) custom-call(s32[2]{0:T(128)} %pad_add_fusion.1.pos_ref, f32[2,2,2,256,256]{4,3,2,1,0:T(8,128)} %pad_maximum_fusion.4.a_ref, f32[2,1024,1024]{2,1,0:T(8,128)} %get-tuple-element.19.x_ref), custom_call_target="tpu_custom_call" | custom-call | tf_op jit(solution)/shard_map/pallas_call | solution.py:306
  646.4 34.5 %shard_map.51 = f32[2,4096,128]{2,1,0:T(8,128)} custom-call(s32[2]{0:T(128)} %pad_add_fusion.1.pos_ref, f32[2,4096,128]{2,1,0:T(8,128)} %get-tuple-element.16.front_ref, f32[2,256,1024]{2,1,0:T(8,128)} %get-tuple-element.20.w_ref, f32[2,256,256]{2,1,0:T(8,128)} %dynamic-slice_select_fusion.own_ref, f32[4,4,2,512,128]{4,3,2,1,0:T(8,128)} %copy-done.1, ...), custom_call_target="tpu_custom_call" | custom-call | tf_op jit(solution)/shard_map/pallas_call | solution.py:374
  (63 shorter events, 30.5 us)
Async XLA Ops:
  80.1 1.7 collective-permute-start.2
  81.8 11.4 %collective-permute-start.3 = (f32[1024,128]{1,0:T(8,128)S(1)}, f32[1024,128]{1,0:T(8,128)S(1)}, u32[]{:S(2)}, u32[]{:S(2)}) collective-permute-start(f32[1024,128]{1,0:T(8,128)S(1)} %collective-permute-done.2), channel_id=1, source_target_pairs={{0,4},{4,0},{8,12},{12,8},{16,20},{20,16},{24,28},{28,24},{32,36},... | collective-permute-start | bytes 1572872 | tf_op jit(solution)/shard_map/ppermute | solution.py:415
  93.2 16.1 %collective-permute-start.14 = (f32[2,512,128]{2,1,0:T(8,128)S(1)}, f32[2,512,128]{2,1,0:T(8,128)S(1)}, u32[]{:S(2)}, u32[]{:S(2)}) collective-permute-start(f32[2,512,128]{2,1,0:T(8,128)S(1)} %get-tuple-element.36), channel_id=1, source_target_pairs={{0,96},{4,100},{8,104},{12,108},{16,112},{20,116},{24,120},{28,124... | collective-permute-start | bytes 1572872 | tf_op jit(solution)/shard_map/ppermute | solution.py:408
  93.8 15.6 %collective-permute-start.12 = (f32[2,512,128]{2,1,0:T(8,128)S(1)}, f32[2,512,128]{2,1,0:T(8,128)S(1)}, u32[]{:S(2)}, u32[]{:S(2)}) collective-permute-start(f32[2,512,128]{2,1,0:T(8,128)S(1)} %get-tuple-element.36), channel_id=1, source_target_pairs={{0,32},{4,36},{8,40},{12,44},{16,48},{20,52},{24,56},{28,60},{32,6... | collective-permute-start | bytes 1572872 | tf_op jit(solution)/shard_map/ppermute | solution.py:407
  96.5 23.9 %collective-permute-start.6 = (f32[2,512,128]{2,1,0:T(8,128)S(1)}, f32[2,512,128]{2,1,0:T(8,128)S(1)}, u32[]{:S(2)}, u32[]{:S(2)}) collective-permute-start(f32[2,512,128]{2,1,0:T(8,128)S(1)} %get-tuple-element.35), channel_id=1, source_target_pairs={{0,24},{4,28},{8,0},{12,4},{16,8},{20,12},{24,16},{28,20},{32,56},... | collective-permute-start | bytes 1572872 | tf_op jit(solution)/shard_map/ppermute | solution.py:408
  109.3 15.7 %collective-permute-start.4 = (f32[2,512,128]{2,1,0:T(8,128)S(1)}, f32[2,512,128]{2,1,0:T(8,128)S(1)}, u32[]{:S(2)}, u32[]{:S(2)}) collective-permute-start(f32[2,512,128]{2,1,0:T(8,128)S(1)} %get-tuple-element.35), channel_id=1, source_target_pairs={{0,8},{4,12},{8,16},{12,20},{16,24},{20,28},{24,0},{28,4},{32,40},... | collective-permute-start | bytes 1572872 | tf_op jit(solution)/shard_map/ppermute | solution.py:407
  109.3 15.7 %collective-permute-start.15 = (f32[2,256,128]{2,1,0:T(8,128)S(1)}, f32[2,256,128]{2,1,0:T(8,128)S(1)}, u32[]{:S(2)}, u32[]{:S(2)}) collective-permute-start(f32[2,256,128]{2,1,0:T(8,128)S(1)} %slice.51), channel_id=1, source_target_pairs={{0,96},{4,100},{8,104},{12,108},{16,112},{20,116},{24,120},{28,124... | collective-permute-start | bytes 786440 | tf_op jit(solution)/shard_map/ppermute | solution.py:410
  109.4 15.6 %collective-permute-start.13 = (f32[2,256,128]{2,1,0:T(8,128)S(1)}, f32[2,256,128]{2,1,0:T(8,128)S(1)}, u32[]{:S(2)}, u32[]{:S(2)}) collective-permute-start(f32[2,256,128]{2,1,0:T(8,128)S(1)} %slice.50), channel_id=1, source_target_pairs={{0,32},{4,36},{8,40},{12,44},{16,48},{20,52},{24,56},{28,60},{32,6... | collective-permute-start | bytes 786440 | tf_op jit(solution)/shard_map/ppermute | solution.py:409
  120.4 11.8 %collective-permute-start.7 = (f32[2,256,128]{2,1,0:T(8,128)S(1)}, f32[2,256,128]{2,1,0:T(8,128)S(1)}, u32[]{:S(2)}, u32[]{:S(2)}) collective-permute-start(f32[2,256,128]{2,1,0:T(8,128)S(1)} %slice.47), channel_id=1, source_target_pairs={{0,24},{4,28},{8,0},{12,4},{16,8},{20,12},{24,16},{28,20},{32,56},... | collective-permute-start | bytes 786440 | tf_op jit(solution)/shard_map/ppermute | solution.py:410
  125.0 8.2 %collective-permute-start.5 = (f32[2,256,128]{2,1,0:T(8,128)S(1)}, f32[2,256,128]{2,1,0:T(8,128)S(1)}, u32[]{:S(2)}, u32[]{:S(2)}) collective-permute-start(f32[2,256,128]{2,1,0:T(8,128)S(1)} %slice.46), channel_id=1, source_target_pairs={{0,8},{4,12},{8,16},{12,20},{16,24},{20,28},{24,0},{28,4},{32,40},... | collective-permute-start | bytes 786440 | tf_op jit(solution)/shard_map/ppermute | solution.py:409
  126.9 119.1 %collective-permute-start.18 = (f32[4,2,512,128]{3,2,1,0:T(8,128)}, f32[4,2,512,128]{3,2,1,0:T(8,128)}, u32[]{:S(2)}, u32[]{:S(2)}) collective-permute-start(f32[4,2,512,128]{3,2,1,0:T(8,128)} %get-tuple-element.34), channel_id=1, source_target_pairs={{0,24},{4,28},{8,0},{12,4},{16,8},{20,12},{24,16},{28,20},{32,56},... | collective-permute-start | bytes 6291464 | tf_op jit(solution)/shard_map/ppermute | solution.py:408
  132.3 115.8 %collective-permute-start.16 = (f32[4,2,512,128]{3,2,1,0:T(8,128)}, f32[4,2,512,128]{3,2,1,0:T(8,128)}, u32[]{:S(2)}, u32[]{:S(2)}) collective-permute-start(f32[4,2,512,128]{3,2,1,0:T(8,128)} %get-tuple-element.34), channel_id=1, source_target_pairs={{0,8},{4,12},{8,16},{12,20},{16,24},{20,28},{24,0},{28,4},{32,40},... | collective-permute-start | bytes 6291464 | tf_op jit(solution)/shard_map/ppermute | solution.py:407
  135.6 116.0 %collective-permute-start.10 = (f32[4,2,512,128]{3,2,1,0:T(8,128)}, f32[4,2,512,128]{3,2,1,0:T(8,128)}, u32[]{:S(2)}, u32[]{:S(2)}) collective-permute-start(f32[4,2,512,128]{3,2,1,0:T(8,128)} %get-tuple-element.32), channel_id=1, source_target_pairs={{0,96},{4,100},{8,104},{12,108},{16,112},{20,116},{24,120},{28,124... | collective-permute-start | bytes 6291464 | tf_op jit(solution)/shard_map/ppermute | solution.py:408
  135.6 118.4 %collective-permute-start.8 = (f32[4,2,512,128]{3,2,1,0:T(8,128)}, f32[4,2,512,128]{3,2,1,0:T(8,128)}, u32[]{:S(2)}, u32[]{:S(2)}) collective-permute-start(f32[4,2,512,128]{3,2,1,0:T(8,128)} %get-tuple-element.32), channel_id=1, source_target_pairs={{0,32},{4,36},{8,40},{12,44},{16,48},{20,52},{24,56},{28,60},{32,6... | collective-permute-start | bytes 6291464 | tf_op jit(solution)/shard_map/ppermute | solution.py:407
  138.9 219.8 %all-to-all-start.1 = ((f32[128,128,128]{2,1,0:T(8,128)}), f32[128,128,128]{2,1,0:T(8,128)}, u32[]{:S(2)}, u32[]{:S(2)}) async-start(f32[128,128,128]{2,1,0:T(8,128)} %bitcast.59), calls=%async_computation.1 | async-start | bytes 16777216 | tf_op jit(solution)/shard_map/all_to_all | solution.py:440
  247.3 41.2 %collective-permute-start.19 = (f32[4,2,256,128]{3,2,1,0:T(8,128)S(1)}, f32[4,2,256,128]{3,2,1,0:T(8,128)}, u32[]{:S(2)}, u32[]{:S(2)}) collective-permute-start(f32[4,2,256,128]{3,2,1,0:T(8,128)S(1)} %slice.53), channel_id=1, source_target_pairs={{0,24},{4,28},{8,0},{12,4},{16,8},{20,12},{24,16},{28,20},{32,56},... | collective-permute-start | bytes 3145736 | tf_op jit(solution)/shard_map/ppermute | solution.py:410
  250.4 41.7 %collective-permute-start.17 = (f32[4,2,256,128]{3,2,1,0:T(8,128)}, f32[4,2,256,128]{3,2,1,0:T(8,128)}, u32[]{:S(2)}, u32[]{:S(2)}) collective-permute-start(f32[4,2,256,128]{3,2,1,0:T(8,128)} %slice.52), channel_id=1, source_target_pairs={{0,8},{4,12},{8,16},{12,20},{16,24},{20,28},{24,0},{28,4},{32,40},... | collective-permute-start | bytes 3145736 | tf_op jit(solution)/shard_map/ppermute | solution.py:409
  254.0 41.2 %collective-permute-start.11 = (f32[4,2,256,128]{3,2,1,0:T(8,128)}, f32[4,2,256,128]{3,2,1,0:T(8,128)}, u32[]{:S(2)}, u32[]{:S(2)}) collective-permute-start(f32[4,2,256,128]{3,2,1,0:T(8,128)} %slice.49), channel_id=1, source_target_pairs={{0,96},{4,100},{8,104},{12,108},{16,112},{20,116},{24,120},{28,124... | collective-permute-start | bytes 3145736 | tf_op jit(solution)/shard_map/ppermute | solution.py:410
  256.3 38.9 %collective-permute-start.9 = (f32[4,2,256,128]{3,2,1,0:T(8,128)}, f32[4,2,256,128]{3,2,1,0:T(8,128)}, u32[]{:S(2)}, u32[]{:S(2)}) collective-permute-start(f32[4,2,256,128]{3,2,1,0:T(8,128)} %slice.48), channel_id=1, source_target_pairs={{0,32},{4,36},{8,40},{12,44},{16,48},{20,52},{24,56},{28,60},{32,6... | collective-permute-start | bytes 3145736 | tf_op jit(solution)/shard_map/ppermute | solution.py:409
  296.9 2.9 copy-start.3
  299.6 5.6 copy-start
  305.3 3.3 copy-start.1
  308.6 45.9 %collective-permute-start.20 = (f32[2,2,1024,128]{3,2,1,0:T(8,128)S(1)}, f32[2,2,1024,128]{3,2,1,0:T(8,128)S(1)}, u32[]{:S(2)}, u32[]{:S(2)}) collective-permute-start(f32[2,2,1024,128]{3,2,1,0:T(8,128)S(1)} %get-tuple-element.30), channel_id=1, source_target_pairs={{0,2},{2,0},{1,3},{3,1},{4,6},{6,4},{5,7},{7,5},{8,10},{10,8},{9,1... | collective-permute-start | bytes 6291464 | tf_op jit(solution)/shard_map/ppermute | solution.py:415
  358.7 41.5 %collective-permute-start.21 = (f32[2,2,2,1024,128]{4,3,2,1,0:T(8,128)}, f32[2,2,2,1024,128]{4,3,2,1,0:T(8,128)}, u32[]{:S(2)}, u32[]{:S(2)}) collective-permute-start(f32[2,2,2,1024,128]{4,3,2,1,0:T(8,128)} %get-tuple-element.28), channel_id=1, source_target_pairs={{0,1},{1,0},{2,3},{3,2},{4,5},{5,4},{6,7},{7,6},{8,9},{9,8},{10,11... | collective-permute-start | bytes 12582920 | tf_op jit(solution)/shard_map/ppermute | solution.py:415
  378.6 15.9 %collective-permute-start = (f32[2,256,256]{2,1,0:T(8,128)}, f32[2,256,256]{2,1,0:T(8,128)S(1)}, u32[]{:S(2)}, u32[]{:S(2)}) collective-permute-start(f32[2,256,256]{2,1,0:T(8,128)} %get-tuple-element.17), channel_id=1, source_target_pairs={{0,2},{2,0},{1,3},{3,1},{4,6},{6,4},{5,7},{7,5},{8,10},{10,8},{9,1... | collective-permute-start | bytes 1572872 | tf_op jit(solution)/shard_map/ppermute | solution.py:415
  395.7 2.7 collective-permute-start.1
  398.5 2.9 copy-start.2
